TPU v7x, 256 devices: a whole 4x4x8 slice. The times are simulated.
256 devices in a mesh: row: 32 (over z, x_hi, core), key: 8 (over y, x_lo).
Axes of the slice: x: 4 (x_hi: 2, x_lo: 2; x = x_hi * 2 + x_lo), y: 4, z: 8, core: 2. Of those that a mesh axis runs over, the one named last changes fastest.
Arguments:
- query: bfloat16 [160, 2048, 128], P('row', 'key'), may hold values from -6 to 6
- key_in: bfloat16 [160, 2048, 128], P('row', 'key'), may hold values from -6 to 6
- value: bfloat16 [160, 2048, 128], P('row', 'key'), may hold values from -6 to 6
- output: bfloat16 [160, 2048, 128], P('row', 'key'), may hold values from -3 to 3
- dout: bfloat16 [160, 2048, 128], P('row', 'key'), may hold values from -192 to 192
- lse: float32 [4, 160, 2048], P(None, 'row', 'key'), may hold values from 8 to 9
- bias: float32 [4, 2048, 2048], P(None, 'key', 'row'), may hold values from -6 to 6
- mask: int32 [2048], replicated, may hold values 0 or 1
Outputs:
- grad_query: float32 [160, 2048, 128], P('row', 'key')
- grad_key: float32 [160, 2048, 128], P('row', 'key')
- grad_value: float32 [160, 2048, 128], P('row', 'key')
- grad_bias: float32 [4, 2048, 2048], P(None, 'key', 'row')
All inputs are finite; a program needn't handle non-finite values.
Results may differ from a plain program's by a relative error of at most 0.011.
Values may be sent and summed in bfloat16 or wider, within the bound.
A program may use at most 128 MiB of HBM per device.

v0:
```python
import jax
import jax.numpy as jnp
from jax import lax
from jax.sharding import PartitionSpec as P


def split_heads(block, head_count):
    return block.reshape(block.shape[0], head_count, block.shape[1] // head_count)


def row_scores(
    q_heads, d_heads, k_heads, v_heads, lse_row, delta_row, bias_piece, keep_piece, score_scale
):
    logits = (
        jnp.einsum("qhd,khd->hqk", q_heads, k_heads, preferred_element_type=jnp.float32)
        * score_scale
        + bias_piece
    )
    row_probs = jnp.where(keep_piece[None, None, :], jnp.exp(logits - lse_row[:, :, None]), 0.0)
    dprobs = jnp.einsum("qhd,khd->hqk", d_heads, v_heads, preferred_element_type=jnp.float32)
    dlogits = row_probs * (dprobs - delta_row[:, :, None])
    return (row_probs, dlogits)


def reduce_bias(partial_bias):
    return lax.psum_scatter(partial_bias, "row", scatter_dimension=2, tiled=True)


def per_device(query, key_in, value, output, dout, lse, bias, mask):
    slab_rows, col_count, feat_width = query.shape
    head_count = lse.shape[0]
    score_scale = (feat_width // head_count) ** (-0.5)
    bias_full = lax.all_gather(bias, "row", axis=2, tiled=True)
    full_len = bias_full.shape[2]
    key_keep = mask == 1
    lse_rows = jnp.transpose(lse, (1, 0, 2))
    delta_rows = jnp.einsum(
        "iqhd,iqhd->ihq",
        dout.reshape(slab_rows, col_count, head_count, -1),
        output.reshape(slab_rows, col_count, head_count, -1),
        preferred_element_type=jnp.float32,
    )
    query_zero = jnp.zeros((slab_rows, col_count, feat_width), jnp.float32)
    bias_zero = jnp.zeros((head_count, col_count, full_len), jnp.float32)
    key_zero = jnp.zeros((slab_rows, full_len, feat_width), jnp.float32)
    state_now = (query_zero, bias_zero, key_zero, key_zero)
    offset = jnp.int32(0)
    k_piece = lax.all_gather(key_in, "key", axis=1, tiled=True)
    v_piece = lax.all_gather(value, "key", axis=1, tiled=True)
    piece_len = k_piece.shape[1]

    def one_row(summed, row_items):
        query_row, dout_row, key_row, value_row, lse_row, delta_row = row_items
        q_heads = split_heads(query_row, head_count)
        d_heads = split_heads(dout_row, head_count)
        k_heads = split_heads(key_row, head_count)
        row_probs, dlogits = row_scores(
            q_heads,
            d_heads,
            k_heads,
            split_heads(value_row, head_count),
            lse_row,
            delta_row,
            bias_full,
            key_keep,
            score_scale,
        )
        dlogits_low = dlogits.astype(jnp.bfloat16)
        results = []
        summed = summed + dlogits
        q_grad = score_scale * jnp.einsum(
            "hqk,khd->qhd", dlogits_low, k_heads, preferred_element_type=jnp.float32
        )
        results.append(q_grad.reshape(col_count, feat_width))
        probs_low = row_probs.astype(jnp.bfloat16)
        k_grad = score_scale * jnp.einsum(
            "hqk,qhd->khd", dlogits_low, q_heads, preferred_element_type=jnp.float32
        )
        v_grad = jnp.einsum("hqk,qhd->khd", probs_low, d_heads, preferred_element_type=jnp.float32)
        results.append(k_grad.reshape(piece_len, feat_width))
        results.append(v_grad.reshape(piece_len, feat_width))
        return (summed, tuple(results))

    summed, results = lax.scan(
        one_row,
        jnp.zeros((head_count, col_count, piece_len), jnp.float32),
        (query, dout, k_piece, v_piece, lse_rows, delta_rows),
    )
    updated = []
    updated.append(state_now[0] + results[0])
    updated.append(summed)
    position = 1
    first_slot = 2
    updated.append(
        lax.dynamic_update_slice_in_dim(state_now[first_slot], results[position], offset, 1)
    )
    updated.append(
        lax.dynamic_update_slice_in_dim(state_now[first_slot + 1], results[position + 1], offset, 1)
    )
    grad_query, partial_bias, partial_key, partial_value = tuple(updated)
    grad_bias = reduce_bias(partial_bias)
    grad_key, grad_value = (
        lax.psum_scatter(partial_key, "key", scatter_dimension=1, tiled=True),
        lax.psum_scatter(partial_value, "key", scatter_dimension=1, tiled=True),
    )
    return (grad_query, grad_key, grad_value, grad_bias)


def solution(mesh):
    in_specs = (
        P("row", "key", None),
        P("row", "key", None),
        P("row", "key", None),
        P("row", "key", None),
        P("row", "key", None),
        P(None, "row", "key"),
        P(None, "key", "row"),
        P(),
    )
    out_specs = (
        P("row", "key", None),
        P("row", "key", None),
        P("row", "key", None),
        P(None, "key", "row"),
    )
    return jax.shard_map(
        per_device, mesh=mesh, in_specs=in_specs, out_specs=out_specs, check_vma=False
    )
```

profile of v0, /device:TPU:3, one launch (start us, length us, event | category | flops | bytes accessed | tf_op | source)
XLA Modules:
  0.0 798.7 jit_solution(16165560260555082103)
XLA Ops:
  7.2 1.8 copy.33
  9.1 1.9 copy.32
  11.1 1.9 copy.34
  13.0 1.1 copy.39
  14.2 1.1 copy.52
  16.2 99.1 %all-gather.6.cloned.1.call-done = f32[4,256,2048]{1,0,2:T(4,128)} async-done(((f32[4,256,64]{1,0,2:T(4,128)}), f32[4,256,2048]{1,0,2:T(4,128)}) %all-gather.6.cloned.1.call-update) | async-done | bytes 8388624 | tf_op jit(solution)/shard_map/all_gather | solution.py:33
  115.3 9.9 %copy.38 = f32[4,256,2048]{2,1,0:T(8,128)} copy(f32[4,256,2048]{1,0,2:T(4,128)} %all-gather.6.cloned.1.call-done) | data formatting | bytes 16777216
  125.2 51.3 %all-gather.4.cloned.1.call-done = bf16[5,2048,128]{1,2,0:T(8,128)(2,1)} async-done(((bf16[5,256,128]{1,2,0:T(8,128)(2,1)}), bf16[5,2048,128]{1,2,0:T(8,128)(2,1)}) %all-gather.4.cloned.1.call-update) | async-done | bytes 2621456 | tf_op jit(solution)/shard_map/all_gather | solution.py:48
  176.6 65.9 %all-gather.8.cloned.1.call-done = bf16[5,2048,128]{1,2,0:T(8,128)(2,1)} async-done(((bf16[5,256,128]{1,2,0:T(8,128)(2,1)}), bf16[5,2048,128]{1,2,0:T(8,128)(2,1)}) %all-gather.8.cloned.1.call-update) | async-done | bytes 2621456 | tf_op jit(solution)/shard_map/all_gather | solution.py:49
  242.4 164.2 %while.17 = (s32[]{:T(128)}, f32[4,256,2048]{2,1,0:T(8,128)}, f32[5,256,128]{2,1,0:T(8,128)}, f32[5,2048,128]{2,1,0:T(8,128)}, f32[5,2048,128]{2,1,0:T(8,128)}, ...) while((s32[]{:T(128)}, f32[4,256,2048]{2,1,0:T(8,128)}, ...), condition=%wide.region_1.2_spmd.clone, body=%wide.region_0.1_spmd.clone.sunk | while | flops 692355072 | bytes 95186624 | solution.py:84
  242.4 1.3 constant_dynamic-slice_fusion.8
  245.3 6.6 exponential_select_fusion.2
  252.0 6.3 select_add_fusion.2
  258.3 2.0 copy-done
  261.4 1.1 constant_dynamic-update-slice_fusion.7
  262.6 3.5 fusion.40
  266.9 4.2 fusion.41
  272.5 1.3 constant_dynamic-slice_fusion.8
  275.4 6.6 exponential_select_fusion.2
  282.0 9.9 %select_add_fusion.2 = (f32[4,256,2048]{2,1,0:T(8,128)}, bf16[4,256,2048]{2,1,0:T(8,128)(2,1)S(1)}) fusion(f32[4,256,2048]{2,1,0:T(8,128)} %get-tuple-element.312, pred[]{:T(512)S(6)} %compare.3, f32[4,256,2048]{2,1,0:T(8,128)} %exponential_select_fusion.2, f32[4,256]{1,0:T(4,128)S(1)} %get-tuple-element.292, bf16[256,4,32]{0,2,1:T(8,128)(2,1)S(1)} %bitcast.79, ...), kind=kOutput, calls=%fused_computation.clone.1 | convolution fusion | flops 144703488 | bytes 29954048 | tf_op jit(solution)/shard_map/while/body/eval_jaxpr/qhd,khd->hqk/dot_general | solution.py:20
  291.9 2.0 copy-done
  296.0 3.5 fusion.40
  300.3 4.2 fusion.41
  305.9 1.3 constant_dynamic-slice_fusion.8
  308.9 6.6 exponential_select_fusion.2
  315.5 9.9 %select_add_fusion.2 = (f32[4,256,2048]{2,1,0:T(8,128)}, bf16[4,256,2048]{2,1,0:T(8,128)(2,1)S(1)}) fusion(f32[4,256,2048]{2,1,0:T(8,128)} %get-tuple-element.312, pred[]{:T(512)S(6)} %compare.3, f32[4,256,2048]{2,1,0:T(8,128)} %exponential_select_fusion.2, f32[4,256]{1,0:T(4,128)S(1)} %get-tuple-element.292, bf16[256,4,32]{0,2,1:T(8,128)(2,1)S(1)} %bitcast.79, ...), kind=kOutput, calls=%fused_computation.clone.1 | convolution fusion | flops 144703488 | bytes 29954048 | tf_op jit(solution)/shard_map/while/body/eval_jaxpr/qhd,khd->hqk/dot_general | solution.py:20
  325.3 2.0 copy-done
  329.5 3.5 fusion.40
  333.8 4.2 fusion.41
  339.4 1.3 constant_dynamic-slice_fusion.8
  342.4 6.6 exponential_select_fusion.2
  349.0 9.9 %select_add_fusion.2 = (f32[4,256,2048]{2,1,0:T(8,128)}, bf16[4,256,2048]{2,1,0:T(8,128)(2,1)S(1)}) fusion(f32[4,256,2048]{2,1,0:T(8,128)} %get-tuple-element.312, pred[]{:T(512)S(6)} %compare.3, f32[4,256,2048]{2,1,0:T(8,128)} %exponential_select_fusion.2, f32[4,256]{1,0:T(4,128)S(1)} %get-tuple-element.292, bf16[256,4,32]{0,2,1:T(8,128)(2,1)S(1)} %bitcast.79, ...), kind=kOutput, calls=%fused_computation.clone.1 | convolution fusion | flops 144703488 | bytes 29954048 | tf_op jit(solution)/shard_map/while/body/eval_jaxpr/qhd,khd->hqk/dot_general | solution.py:20
  358.9 2.0 copy-done
  362.0 1.1 constant_dynamic-update-slice_fusion.7
  363.0 3.5 fusion.40
  367.4 4.2 fusion.41
  373.0 1.3 constant_dynamic-slice_fusion.8
  375.9 6.6 exponential_select_fusion.2
  382.5 9.9 %select_add_fusion.2 = (f32[4,256,2048]{2,1,0:T(8,128)}, bf16[4,256,2048]{2,1,0:T(8,128)(2,1)S(1)}) fusion(f32[4,256,2048]{2,1,0:T(8,128)} %get-tuple-element.312, pred[]{:T(512)S(6)} %compare.3, f32[4,256,2048]{2,1,0:T(8,128)} %exponential_select_fusion.2, f32[4,256]{1,0:T(4,128)S(1)} %get-tuple-element.292, bf16[256,4,32]{0,2,1:T(8,128)(2,1)S(1)} %bitcast.79, ...), kind=kOutput, calls=%fused_computation.clone.1 | convolution fusion | flops 144703488 | bytes 29954048 | tf_op jit(solution)/shard_map/while/body/eval_jaxpr/qhd,khd->hqk/dot_general | solution.py:20
  392.4 2.0 copy-done
  395.5 1.1 constant_dynamic-update-slice_fusion.7
  396.6 3.5 fusion.40
  400.9 4.2 fusion.41
  405.5 1.1 constant_dynamic-update-slice_fusion.8
  407.2 8.7 %copy.42 = f32[4,256,2048]{1,2,0:T(8,128)} copy(f32[4,256,2048]{2,1,0:T(8,128)} %get-tuple-element.77) | data formatting | bytes 16777216 | tf_op jit(solution)/shard_map/while | solution.py:84
  416.0 104.9 %reduce-scatter.4.cloned.1.call-done = f32[5,256,128]{2,1,0:T(8,128)} async-done(((f32[5,2048,128]{2,1,0:T(8,128)}), f32[5,256,128]{2,1,0:T(8,128)}) %reduce-scatter.4.cloned.1.call-update) | async-done | bytes 655376 | tf_op jit(solution)/shard_map/reduce_scatter | solution.py:103
  520.9 116.5 %reduce-scatter.6.cloned.1.call-done = f32[5,256,128]{2,1,0:T(8,128)} async-done(((f32[5,2048,128]{2,1,0:T(8,128)}), f32[5,256,128]{2,1,0:T(8,128)}) %reduce-scatter.6.cloned.1.call-update) | async-done | bytes 655376 | tf_op jit(solution)/shard_map/reduce_scatter | solution.py:104
  637.4 154.5 %reduce-scatter.8.cloned.1.call-done = f32[4,256,64]{1,2,0:T(8,128)} async-done(((f32[4,256,2048]{1,2,0:T(8,128)}), f32[4,256,64]{1,2,0:T(8,128)}) %reduce-scatter.8.cloned.1.call-update) | async-done | bytes 262160 | tf_op jit(solution)/shard_map/reduce_scatter | solution.py:26
  (74 shorter events, 27.5 us)
Async XLA Ops:
  7.2 108.1 %all-gather.6.cloned.1.call-start = ((), (), s32[]{:S(2)}) async-start(), calls=%async_computation.4 | async-start | bytes 8650752 | tf_op jit(solution)/shard_map/all_gather | solution.py:33
  9.1 167.5 %all-gather.4.cloned.1.call-start = ((), (), s32[]{:S(2)}) async-start(), calls=%async_computation.3 | async-start | bytes 2949120 | tf_op jit(solution)/shard_map/all_gather | solution.py:48
  11.0 231.4 %all-gather.8.cloned.1.call-start = ((), (), s32[]{:S(2)}) async-start(), calls=%async_computation.5 | async-start | bytes 2949120 | tf_op jit(solution)/shard_map/all_gather | solution.py:49
  12.9 507.9 %reduce-scatter.4.cloned.1.call-start = ((), (), s32[]{:S(2)}) async-start(), calls=%async_computation.6 | async-start | bytes 5898240 | tf_op jit(solution)/shard_map/reduce_scatter | solution.py:103
  258.3 2.0 copy-start
  291.9 2.0 copy-start
  325.3 2.0 copy-start
  358.9 2.0 copy-start
  392.4 2.0 copy-start
  406.6 230.8 %reduce-scatter.6.cloned.1.call-start = ((), (), s32[]{:S(2)}) async-start(), calls=%async_computation.7 | async-start | bytes 5898240 | tf_op jit(solution)/shard_map/reduce_scatter | solution.py:104
  407.2 384.7 %reduce-scatter.8.cloned.1.call-start = ((), (), s32[]{:S(2)}) async-start(), calls=%async_computation.8 | async-start | bytes 8650752 | tf_op jit(solution)/shard_map/reduce_scatter | solution.py:26
Sparse Core Ops, SparseCore 0:
  11.4 103.8 all-gather.5
  117.6 58.9 all-gather.3
  178.9 63.5 all-gather.7
  406.7 114.0 reduce-scatter.3
  523.8 113.5 reduce-scatter.5
  642.2 149.6 reduce-scatter.7
where the time goes:
time: 806 us; the launch traced here: 799 us
  waiting for transfers between devices  593 us (74%)
  matrix products  122 us (15%)
  local copies, waits for them, and re-layouts  68.8 us (9%)
  between operations  14.2 us (2%)
    reduce_scatter x1, waiting for transfers between devices, reduce_bias(): lax.psum_scatter(partial_bias, 'row', scatter_dimension=2, tiled=True)  154 us
    reduce_scatter x1, waiting for transfers between devices, per_device(): lax.psum_scatter(partial_value, 'key', scatter_dimension=1, tiled=True)  117 us
    reduce_scatter x1, waiting for transfers between devices, per_device(): lax.psum_scatter(partial_key, 'key', scatter_dimension=1, tiled=True)  105 us
    all_gather x1, waiting for transfers between devices, per_device(): bias_full = lax.all_gather(bias, 'row', axis=2, tiled=True)  99.1 us
    all_gather x1, waiting for transfers between devices, per_device(): v_piece = lax.all_gather(value, 'key', axis=1, tiled=True)  65.9 us
    all_gather x1, waiting for transfers between devices, per_device(): k_piece = lax.all_gather(key_in, 'key', axis=1, tiled=True)  51.3 us
    dot_general x5, matrix products, row_scores(): jnp.einsum('qhd,khd->hqk', d_heads, v_heads, preferred_element_type=jnp.f...  45.7 us
    dot_general x5, matrix products, row_scores(): jnp.einsum('qhd,khd->hqk', q_heads, k_heads, preferred_element_type=jnp.f...  33.1 us
  transfers between devices with their start and end apart: 6, of which 6 were waited for; matrix products, arithmetic and copies ran while one was open for 3% of the time, Pallas kernels for 0%

commit v1 on v0

v1 whole, which is shorter than its diff:
```python
import jax
import jax.numpy as jnp
from jax import lax
from jax.experimental import pallas as pl
from jax.experimental.pallas import tpu as pltpu
from jax.sharding import PartitionSpec as P

MESH = pl.DeviceIdType.MESH
f32, bf16 = jnp.float32, jnp.bfloat16

H, DH, NR = 4, 32, 5
QB = 256
NY, NZ = 4, 8
NJ = NY * QB
KB = 128
JT = 512
SHIFT = 6.0
LOG2E = 1.4426950408889634
SCALE = DH**-0.5
NEG = -1e30


def pieces(a):
    first = a.astype(bf16).astype(f32)
    rest = a - first
    second = rest.astype(bf16).astype(f32)
    return first, second, rest - second


def aligned(start, size):
    return pl.ds(pl.multiple_of(start, size), size)


def kernel(
    q_ref, k_ref, v_ref, o_ref, do_ref, lse_ref, bias_ref, mask_ref,
    gq_ref, gk_ref, gv_ref, gb_ref,
    se, sx, sy, er, xr, yr, lt, gb, own, sr, sl, rr, rl, gqa, sg, gkvr, gqc, sgq, gqr, xs, xg, sb, gbr,
    e_s, e_r, x_s, x_r, c_s, c_r, y_s, y_r, h_s, h_r, fr_s, fr_r, fl_s, fl_r,
    rr_s, rr_r, rl_s, rl_r, g_s, g_r, qc_s, qc_r, qy_s, qy_r, xg_s, xg_r, b_s, b_r, loc,
):
    r, b = lax.axis_index("row"), lax.axis_index("key")
    z, xh, c = r // 4, (r // 2) % 2, r % 2
    y, xl = b // 2, b % 2

    def row_of(zz, xx, cc):
        return zz * 4 + xx * 2 + cc

    def remote(src, dst, s_sem, r_sem, row, key):
        return pltpu.make_async_remote_copy(
            src_ref=src, dst_ref=dst, send_sem=s_sem, recv_sem=r_sem,
            device_id=(row, key), device_id_type=MESH,
        )

    right = row_of((z + 1) % NZ, xh, c)
    left = row_of((z + NZ - 1) % NZ, xh, c)
    across = row_of(z, 1 - xh, c)
    other = row_of(z, xh, 1 - c)
    sends = []

    barrier = pltpu.get_barrier_semaphore()
    for row in (right, left, across):
        pl.semaphore_signal(barrier, inc=1, device_id=(row, b), device_id_type=MESH)
    for n in range(1, 16):
        dy, dc, dx = n // 4, (n // 2) % 2, n % 2
        pl.semaphore_signal(
            barrier, inc=1,
            device_id=(row_of(z, xh, c ^ dc), ((y + dy) % NY) * 2 + (xl ^ dx)),
            device_id_type=MESH,
        )

    for h in range(H):
        se[h] = jnp.exp(bias_ref[h] + SHIFT).T.astype(bf16)

    pl.semaphore_wait(barrier, 18)

    mine = pl.ds(pl.multiple_of(xh * 64, 64), 64)
    lanes = aligned(y * QB, QB)
    rows = pl.ds(c * NR, NR)

    e_copies = []
    for d in range(1, NY):
        yy = (y + d) % NY
        cp = remote(se.at[yy], er.at[z, mine, lanes], e_s.at[d], e_r.at[d], r, yy * 2 + xl)
        cp.start()
        e_copies.append(cp)
    e_own = pltpu.make_async_copy(se.at[y], er.at[z, mine, lanes], loc.at[0])
    e_own.start()

    place = lax.broadcasted_iota(jnp.int32, (16, QB), 0)

    def prep_x(i, carry):
        qt = q_ref[i].astype(f32).T
        dot_ = do_ref[i].astype(f32)
        dt = dot_.T
        prod = (dot_ * o_ref[i].astype(f32)).T
        for h in range(H):
            hs = slice(h * DH, (h + 1) * DH)
            l1, l2, l3 = pieces((lse_ref[h, pl.ds(i, 1), :] + SHIFT) * LOG2E)
            d1, d2, d3 = pieces(jnp.sum(prod[hs], axis=0, keepdims=True))
            aux = jnp.where(place == 6, 1.0, 0.0)
            for n, piece in enumerate((l1, l2, l3, d1, d2, d3)):
                aux = jnp.where(place == n, piece, aux)
            sx[h, i, 0:32] = qt[hs].astype(bf16)
            sx[h, i, 32:64] = dt[hs].astype(bf16)
            sx[h, i, 64:80] = aux.astype(bf16)
        return carry

    lax.fori_loop(0, NR, prep_x, 0)

    x_copies = []
    for d in range(1, NY):
        yy = (y + d) % NY
        cp = remote(sx.at[yy], xr.at[rows, 32:112, lanes], x_s.at[d], x_r.at[d], r, yy * 2 + xl)
        cp.start()
        x_copies.append(cp)
    x_own = pltpu.make_async_copy(sx.at[y], xr.at[rows, 32:112, lanes], loc.at[1])
    x_own.start()

    for cp in e_copies:
        cp.wait_recv()
    e_own.wait()
    h_copy = remote(er.at[z, mine], er.at[z, mine], h_s, h_r, across, b)
    h_copy.start()

    def prep_y(i, carry):
        for ref, lo in ((k_ref, 0), (v_ref, 32)):
            full = ref[i].astype(f32)
            for cc in range(2):
                part = jnp.concatenate(
                    [full[cc * 64 : cc * 64 + 64], full[128 + cc * 64 : 192 + cc * 64]], 0
                ).T
                for h in range(H):
                    sy[h, cc, i, lo : lo + 32] = part[h * DH : (h + 1) * DH].astype(bf16)
        return carry

    lax.fori_loop(0, NR, prep_y, 0)

    y_copies = []
    for n in range(1, 16):
        dy, dc, dx = n // 4, (n // 2) % 2, n % 2
        yy, cc = (y + dy) % NY, c ^ dc
        cp = remote(
            sy.at[yy, cc], yr.at[b, rows], y_s.at[n], y_r.at[n],
            row_of(z, xh, cc), yy * 2 + (xl ^ dx),
        )
        cp.start()
        y_copies.append(cp)
    y_own = pltpu.make_async_copy(sy.at[y, c], yr.at[b, rows], loc.at[2])
    y_own.start()

    h_copy.wait_recv()

    def ring(step):
        going_r, going_l = (z + NZ - step) % NZ, (z + step) % NZ
        if step < 3:
            src_r, src_l = er.at[going_r], er.at[going_l]
        else:
            src_r, src_l = er.at[going_r, 0:64], er.at[going_l, 64:128]
        cr = remote(src_r, src_r, fr_s.at[step], fr_r.at[step], right, b)
        cl = remote(src_l, src_l, fl_s.at[step], fl_r.at[step], left, b)
        cr.start()
        cl.start()
        return cr, cl

    ring_copies = [ring(0)]

    c_copies = []
    x_own.wait()
    for d in range(NY):
        if d:
            x_copies[d - 1].wait_recv()
        part = xr.at[rows, 32:112, aligned(((y + NY - d) % NY) * QB, QB)]
        cp = remote(part, part, c_s.at[d], c_r.at[d], other, b)
        cp.start()
        c_copies.append(cp)

    for step in range(1, 4):
        for cp in ring_copies[-1]:
            cp.wait_recv()
        ring_copies.append(ring(step))

    gqa[...] = jnp.zeros_like(gqa)
    for cp in c_copies:
        cp.wait_recv()

    def twice(i, carry):
        xr[i, 0:32, :] = xr[i, 32:64, :]
        xr[i, 112:128, :] = jnp.zeros((16, NJ), bf16)
        return carry

    lax.fori_loop(0, 2 * NR, twice, 0)
    for cp in y_copies:
        cp.wait_recv()
    y_own.wait()
    for cp in ring_copies[-1]:
        cp.wait_recv()

    spot = lax.broadcasted_iota(jnp.int32, (32, 2 * KB), 0)

    def score_rows(m, z_a, z_b):
        gb[...] = jnp.zeros_like(gb)
        neg = jnp.concatenate([mask_ref[c, z_a], mask_ref[c, z_b]], 1)
        aux_t = jnp.where(spot < 3, -1.0, jnp.where(spot == 6, neg, 0.0)).astype(bf16)
        aux_d = jnp.where((spot >= 3) & (spot < 6), -1.0, 0.0).astype(bf16)
        zero = jnp.zeros((32, 2 * KB), bf16)

        def one_row(i, carry):
            both = jnp.concatenate([yr[z_a, i], yr[z_b, i]], 1)
            kt, vt = both[0:32], both[32:64]
            scaled = kt.astype(f32) * (SCALE * LOG2E)
            high = scaled.astype(bf16)
            low = (scaled - high.astype(f32)).astype(bf16)
            lhs_t = jnp.concatenate([high, low, zero, aux_t], 0)
            lhs_d = jnp.concatenate([zero, zero, vt, aux_d], 0)
            lt[...] = jnp.concatenate([lhs_t, lhs_d], 1).T
            gk = gv = None
            for jt in range(NJ // JT):
                js = slice(jt * JT, (jt + 1) * JT)
                x = xr[i, :, js]
                td = jnp.dot(lt[...], x, preferred_element_type=f32)
                e = jnp.concatenate([er[z_a, :, js], er[z_b, :, js]], 0).astype(f32)
                p = jnp.exp2(td[: 2 * KB]) * e
                ds = p * td[2 * KB :]
                gb[:, js] += ds
                pb, db = p.astype(bf16), ds.astype(bf16)
                last = (((1,), (1,)), ((), ()))
                gvj = lax.dot_general(x[64:96], pb, last, preferred_element_type=f32)
                gkj = lax.dot_general(x[0:32], db, last, preferred_element_type=f32)
                gk, gv = (gkj, gvj) if jt == 0 else (gk + gkj, gv + gvj)
                gqa[i, :, js] += jnp.dot(kt, db, preferred_element_type=f32)
            out = jnp.concatenate([gk * SCALE, gv], 0).astype(bf16)
            sg[m, 0, i] = out[:, :KB]
            sg[m, 1, i] = out[:, KB:]
            return carry

        lax.fori_loop(0, 2 * NR, one_row, 0, unroll=2)

    me = y * 4 + c * 2 + xl

    def return_keys(m, half, zz):
        for cc in range(2):
            is_self = (zz == b) & (c == cc)
            src, dst = sg.at[m, half, cc * NR : (cc + 1) * NR], gkvr.at[me]

            @pl.when(jnp.logical_not(is_self))
            def _():
                remote(src, dst, g_s.at[m, half, cc], g_r.at[me], row_of(z, xh, cc), zz).start()

            @pl.when(is_self)
            def _():
                cp = pltpu.make_async_copy(src, dst, loc.at[3])
                cp.start()
                cp.wait()

    def drain_keys(m, half, zz):
        for cc in range(2):
            is_self = (zz == b) & (c == cc)
            src, dst = sg.at[m, half, cc * NR : (cc + 1) * NR], gkvr.at[me]

            @pl.when(jnp.logical_not(is_self))
            def _():
                remote(src, dst, g_s.at[m, half, cc], g_r.at[me], row_of(z, xh, cc), zz).wait_send()

    blocks = [((z + 4 - m) % NZ, (z + 4 + m) % NZ if m else z) for m in range(4)]
    rs_copies = []
    for m in range(4):
        z_a, z_b = blocks[m]
        score_rows(m, z_a, z_b)
        if m == 0:
            own[...] = gb[KB:, :]
            sr[0, 0:64] = gb[0:64, :].astype(bf16)
            sl[0, 64:128] = gb[64:128, :].astype(bf16)
            cr = remote(sr.at[0, 0:64], rr.at[0, 0:64], rr_s.at[0], rr_r.at[0], right, b)
            cl = remote(sl.at[0, 64:128], rl.at[0, 64:128], rl_s.at[0], rl_r.at[0], left, b)
        else:
            for cp in rs_copies[-1]:
                cp.wait_recv()
            if m == 1:
                sr[m, 0:64] = (gb[0:64, :] + rr[0, 0:64].astype(f32)).astype(bf16)
                sr[m, 64:128] = gb[64:128, :].astype(bf16)
                sl[m, 0:64] = gb[128:192, :].astype(bf16)
                sl[m, 64:128] = (gb[192:256, :] + rl[0, 64:128].astype(f32)).astype(bf16)
            else:
                sr[m] = (gb[0:KB, :] + rr[m - 1].astype(f32)).astype(bf16)
                sl[m] = (gb[KB:, :] + rl[m - 1].astype(f32)).astype(bf16)
            cr = remote(sr.at[m], rr.at[m], rr_s.at[m], rr_r.at[m], right, b)
            cl = remote(sl.at[m], rl.at[m], rl_s.at[m], rl_r.at[m], left, b)
        cr.start()
        cl.start()
        rs_copies.append((cr, cl))
        return_keys(m, 0, z_a)
        return_keys(m, 1, z_b)

    theirs = pl.ds((1 - c) * NR, NR)
    qc_copy = remote(gqa.at[theirs], gqc, qc_s, qc_r, other, b)
    qc_copy.start()
    qc_copy.wait_recv()

    def add_q(i, carry):
        total = ((gqa[c * NR + i] + gqc[i]) * SCALE).astype(bf16)
        for n in range(NY):
            sgq[n, i] = total[:, n * QB : (n + 1) * QB]
        return carry

    lax.fori_loop(0, NR, add_q, 0)
    q_copies = []
    for d in range(1, NY):
        yy = (y + d) % NY
        cp = remote(sgq.at[yy], gqr.at[y], qy_s.at[d], qy_r.at[d], r, yy * 2 + xl)
        cp.start()
        q_copies.append(cp)
    gqr[y] = sgq[y]

    for cp in rs_copies[-1]:
        cp.wait_recv()
    across_rows = pl.ds(pl.multiple_of((1 - xh) * 64, 64), 64)
    xs[...] = (
        own[across_rows, :] + rr[3, across_rows, :].astype(f32) + rl[3, across_rows, :].astype(f32)
    ).astype(bf16)
    xg_copy = remote(xs, xg, xg_s, xg_r, across, b)
    xg_copy.start()
    own[mine, :] = own[mine, :] + rr[3, mine, :].astype(f32) + rl[3, mine, :].astype(f32)

    for n in range(16):

        @pl.when(n != me)
        def _(n=n):
            remote(sg.at[0, 0, 0:NR], gkvr.at[n], g_s.at[0, 0, 0], g_r.at[n], r, b).wait_recv()

    def keys_home(i, carry):
        for cc in range(2):
            for ref, lo in ((gk_ref, 0), (gv_ref, 32)):
                heads = [
                    gkvr[h * 4 + cc * 2, i, lo : lo + 32].astype(f32)
                    + gkvr[h * 4 + cc * 2 + 1, i, lo : lo + 32].astype(f32)
                    for h in range(H)
                ]
                part = jnp.concatenate(heads, 0).T
                ref[i, cc * 64 : cc * 64 + 64] = part[0:64]
                ref[i, 128 + cc * 64 : 192 + cc * 64] = part[64:128]
        return carry

    lax.fori_loop(0, NR, keys_home, 0)

    xg_copy.wait_recv()
    total = (own[mine, :] + xg[...].astype(f32)).astype(bf16)
    for n in range(NY):
        sb[n] = total[:, n * QB : (n + 1) * QB]
    b_copies = []
    for d in range(1, NY):
        yy = (y + d) % NY
        cp = remote(sb.at[yy], gbr.at[y], b_s.at[d], b_r.at[d], r, yy * 2 + xl)
        cp.start()
        b_copies.append(cp)
    gbr[y] = sb[y]

    for cp in q_copies:
        cp.wait_recv()

    def query_home(i, carry):
        gq_ref[i] = jnp.concatenate([gqr[h, i].astype(f32) for h in range(H)], 0).T
        return carry

    lax.fori_loop(0, NR, query_home, 0)

    for cp in b_copies:
        cp.wait_recv()
    for h in range(H):
        gb_ref[h] = gbr[h].astype(f32).T

    for m in range(4):
        drain_keys(m, 0, blocks[m][0])
        drain_keys(m, 1, blocks[m][1])
    for cp in [h_copy, qc_copy, xg_copy, *e_copies, *x_copies, *y_copies, *c_copies, *q_copies, *b_copies]:
        cp.wait_send()
    for pair in (*ring_copies, *rs_copies):
        for cp in pair:
            cp.wait_send()


def per_device(query, key_in, value, output, dout, lse, bias, mask):
    neg = jnp.where(mask == 1, 0.0, NEG).astype(f32)
    neg = neg.reshape(NZ, 2, 2, 64).transpose(2, 0, 1, 3).reshape(2, NZ, 1, KB)
    dma = pltpu.SemaphoreType.DMA
    grad = jax.ShapeDtypeStruct(query.shape, f32)
    vmem = pl.BlockSpec(memory_space=pltpu.VMEM)
    scratch = [
        pltpu.VMEM((H, 64, QB), bf16),
        pltpu.VMEM((H, NR, 80, QB), bf16),
        pltpu.VMEM((H, 2, NR, 64, KB), bf16),
        pltpu.VMEM((NZ, KB, NJ), bf16),
        pltpu.VMEM((2 * NR, 128, NJ), bf16),
        pltpu.VMEM((NZ, 2 * NR, 64, KB), bf16),
        pltpu.VMEM((4 * KB, 128), bf16),
        pltpu.VMEM((2 * KB, NJ), f32),
        pltpu.VMEM((KB, NJ), f32),
        pltpu.VMEM((4, KB, NJ), bf16),
        pltpu.VMEM((4, KB, NJ), bf16),
        pltpu.VMEM((4, KB, NJ), bf16),
        pltpu.VMEM((4, KB, NJ), bf16),
        pltpu.VMEM((2 * NR, DH, NJ), f32),
        pltpu.VMEM((4, 2, 2 * NR, 64, KB), bf16),
        pltpu.VMEM((16, NR, 64, KB), bf16),
        pltpu.VMEM((NR, DH, NJ), f32),
        pltpu.VMEM((NY, NR, DH, QB), bf16),
        pltpu.VMEM((NY, NR, DH, QB), bf16),
        pltpu.VMEM((64, NJ), bf16),
        pltpu.VMEM((64, NJ), bf16),
        pltpu.VMEM((NY, 64, QB), bf16),
        pltpu.VMEM((NY, 64, QB), bf16),
    ]
    sems = [
        dma((4,)), dma((4,)), dma((4,)), dma((4,)), dma((4,)), dma((4,)), dma((16,)), dma((16,)),
        dma, dma, dma((4,)), dma((4,)), dma((4,)), dma((4,)),
        dma((4,)), dma((4,)), dma((4,)), dma((4,)), dma((4, 2, 2)), dma((16,)), dma, dma,
        dma((4,)), dma((4,)), dma, dma, dma((4,)), dma((4,)), dma((4,)),
    ]
    return pl.pallas_call(
        kernel,
        out_shape=[grad, grad, grad, jax.ShapeDtypeStruct(bias.shape, f32)],
        in_specs=[vmem] * 8,
        out_specs=[vmem] * 4,
        scratch_shapes=scratch + sems,
        compiler_params=pltpu.CompilerParams(
            collective_id=0, has_side_effects=True, vmem_limit_bytes=56 << 20
        ),
    )(query, key_in, value, output, dout, lse, bias, neg)


def solution(mesh):
    in_specs = (
        P("row", "key", None),
        P("row", "key", None),
        P("row", "key", None),
        P("row", "key", None),
        P("row", "key", None),
        P(None, "row", "key"),
        P(None, "key", "row"),
        P(),
    )
    out_specs = (
        P("row", "key", None),
        P("row", "key", None),
        P("row", "key", None),
        P(None, "key", "row"),
    )
    return jax.shard_map(
        per_device, mesh=mesh, in_specs=in_specs, out_specs=out_specs, check_vma=False
    )
```

time: 806 us -> 115 us (0.14)
  waiting for transfers between devices: 593 us -> 0 us
  matrix products: 122 us -> 0 us
  Pallas kernels: 0 us -> 104 us
  local copies, waits for them, and re-layouts: 68.8 us -> 8.85 us
  between operations: 14.2 us -> 0.66 us
    reduce_scatter x3 -> x0, waiting for transfers between devices: 376 us -> none  [the longest x1 154 us: reduce_bias(): lax.psum_scatter(partial_bias, 'row', scatter_dimension=2, tiled=True)]
    all_gather x3 -> x0, waiting for transfers between devices: 216 us -> none  [the longest x1 99.1 us: per_device(): bias_full = lax.all_gather(bias, 'row', axis=2, tiled=True)]
    dot_general x25 -> x0, matrix products: 122 us -> none  [the longest x5 45.7 us: row_scores(): jnp.einsum('qhd,khd->hqk', d_heads, v_heads, preferred_element_type=jnp.f...]
    pallas_call x0 -> x1, Pallas kernels: none -> 104 us  [per_device(): pl.pallas_call(kernel, out_shape=[grad, grad, grad, jax.ShapeDtypeStruct(...]
    while x11 -> x0, local copies, waits for them, and re-layouts: 18.5 us -> none
    dynamic_update_slice x30 -> x0, local copies, waits for them, and re-layouts: 17.9 us -> none  [per_device(): lax.scan(one_row, jnp.zeros((head_count, col_count, piece_len), jnp.float...]
    unnamed x6 -> x13, local copies, waits for them, and re-layouts: 17.8 us -> 6.08 us
    dynamic_slice x20 -> x0, local copies, waits for them, and re-layouts: 11.1 us -> none  [per_device(): lax.scan(one_row, jnp.zeros((head_count, col_count, piece_len), jnp.float...]
  transfers between devices with their start and end apart: 6 -> 0, of which waited for: 6 -> 0; matrix products, arithmetic and copies ran while one was open for 3% -> 0% of each run, Pallas kernels for 0% -> 0%
where the time goes in v1:
time: 115 us; the launch traced here: 114 us
  Pallas kernels  104 us (90%)
  local copies, waits for them, and re-layouts  8.85 us (8%)
    pallas_call x1, Pallas kernels, per_device(): pl.pallas_call(kernel, out_shape=[grad, grad, grad, jax.ShapeDtypeStruct(...  104 us
    unnamed x13, local copies, waits for them, and re-layouts  6.08 us

profile of v1, /device:TPU:3, one launch (start us, length us, event | category | flops | bytes accessed | tf_op | source)
XLA Modules:
  0.0 114.3 jit_solution(1672393899487253218)
XLA Ops:
  0.6 0.7 compare_select_fusion
  1.3 0.1 reshape.14
  1.4 0.0 copy-start.3
  1.4 0.7 reshape.15.mask_ref
  2.1 0.0 copy-done.3
  2.1 0.6 copy.16.lse_ref
  2.8 1.9 %copy.17.bias_ref = f32[4,256,64]{2,1,0:T(8,128)} copy(f32[4,256,64]{1,2,0:T(8,128)} %param.14) | data formatting | bytes 524288 | tf_op args[6]
  4.7 104.1 %shard_map.111 = (f32[5,256,128]{2,1,0:T(8,128)}, f32[5,256,128]{2,1,0:T(8,128)}, f32[5,256,128]{2,1,0:T(8,128)}, f32[4,256,64]{2,1,0:T(8,128)}) custom-call(bf16[5,256,128]{2,1,0:T(8,128)(2,1)} %q_ref.1, bf16[5,256,128]{2,1,0:T(8,128)(2,1)} %k_ref.1, bf16[5,256,128]{2,1,0:T(8,128)(2,1)} %v_ref.1, bf16[5,256,128]{2,1,0:T(8,128)(2,1)} %o_ref.1, ...), custom_call_target="tpu_custom_call" | custom-call | tf_op jit(solution)/shard_map/pallas_call | solution.py:418
  108.8 0.0 copy-start.2
  108.8 2.0 %copy.18 = f32[4,256,64]{1,2,0:T(8,128)} copy(f32[4,256,64]{2,1,0:T(8,128)} %get-tuple-element.11) | data formatting | bytes 524288 | tf_op jit(solution)/shard_map/pallas_call | solution.py:418
  110.8 0.0 copy-done.2
  110.8 0.0 copy-start.1
  110.8 0.8 copy.22
  111.7 0.5 copy-done.1
  112.1 0.0 copy-start
  112.1 0.8 copy.23
  113.0 0.5 copy-done
  113.5 0.8 copy.24
  (1 shorter events, 0.0 us)
Async XLA Ops:
  1.4 0.7 copy-start.3
  108.8 2.0 %copy-start.2 = (f32[5,256,128]{2,1,0:T(8,128)S(1)}, f32[5,256,128]{2,1,0:T(8,128)}, u32[]{:S(2)}) copy-start(f32[5,256,128]{2,1,0:T(8,128)} %get-tuple-element.16) | copy-start | bytes 1966084
  110.8 1.3 %copy-start.1 = (f32[5,256,128]{2,1,0:T(8,128)S(1)}, f32[5,256,128]{2,1,0:T(8,128)}, u32[]{:S(2)}) copy-start(f32[5,256,128]{2,1,0:T(8,128)} %get-tuple-element.17) | copy-start | bytes 1966084
  112.1 1.3 %copy-start = (f32[5,256,128]{2,1,0:T(8,128)S(1)}, f32[5,256,128]{2,1,0:T(8,128)}, u32[]{:S(2)}) copy-start(f32[5,256,128]{2,1,0:T(8,128)} %get-tuple-element.18) | copy-start | bytes 1966084

commit v2 on v0

v2 whole, which is shorter than its diff:
```python
import jax
import jax.numpy as jnp
from jax import lax
from jax.experimental import pallas as pl
from jax.experimental.pallas import tpu as pltpu
from jax.sharding import PartitionSpec as P

MESH = pl.DeviceIdType.MESH
f32, bf16 = jnp.float32, jnp.bfloat16

H, DH, NR = 4, 32, 5
QB = 256
NY, NZ = 4, 8
NJ = NY * QB
HJ = NJ // 2
KB = 128
SHIFT = 6.0
LOG2E = 1.4426950408889634
SCALE = DH**-0.5
NEG = -1e30


def pieces(a):
    first = a.astype(bf16).astype(f32)
    rest = a - first
    second = rest.astype(bf16).astype(f32)
    return first, second, rest - second


def aligned(start, size):
    return pl.ds(pl.multiple_of(start, size), size)


def kernel(
    q_ref, k_ref, v_ref, o_ref, do_ref, lse_ref, bias_ref, mask_ref,
    gqr, gkvr, gbr,
    se, sx, sy, er, xr, yr, neg, lt, gb, own, sr, sl, rr, rl, gqa, gka, sg, pr, gqc, sgq, sb,
    e_s, e_r, x_s, x_r, c_s, c_r, y_s, y_r, w_s, w_r, fr_s, fr_r, fl_s, fl_r,
    rr_s, rr_r, rl_s, rl_r, p_s, p_r, g_s, g_r, qc_s, qc_r, qy_s, qy_r, b_s, b_r, loc,
):
    r, b = lax.axis_index("row"), lax.axis_index("key")
    z, xh, c = r // 4, (r // 2) % 2, r % 2
    y, xl = b // 2, b % 2

    def row_of(zz, xx, cc):
        return zz * 4 + xx * 2 + cc

    def remote(src, dst, s_sem, r_sem, row, key):
        return pltpu.make_async_remote_copy(
            src_ref=src, dst_ref=dst, send_sem=s_sem, recv_sem=r_sem,
            device_id=(row, key), device_id_type=MESH,
        )

    right = row_of((z + 1) % NZ, xh, c)
    left = row_of((z + NZ - 1) % NZ, xh, c)
    across = row_of(z, 1 - xh, c)
    other = row_of(z, xh, 1 - c)
    done = []

    barrier = pltpu.get_barrier_semaphore()
    greet = [(right, b), (left, b)]
    greet += [(across, ((y + d) % NY) * 2 + xl) for d in range(NY)]
    greet += [
        (row_of(z, xh, c ^ ((n // 2) % 2)), ((y + n // 4) % NY) * 2 + (xl ^ (n % 2)))
        for n in range(1, 16)
    ]
    for device in greet:
        pl.semaphore_signal(barrier, inc=1, device_id=device, device_id_type=MESH)

    for h in range(H):
        se[h] = jnp.exp(bias_ref[h] + SHIFT).astype(bf16)

    pl.semaphore_wait(barrier, len(greet))

    mine = aligned(xh * 64, 64)
    lanes = aligned(y * QB, QB)
    lanes_e = aligned((y % 2) * QB, QB)
    rows = pl.ds(c * NR, NR)

    e_place = er.at[y // 2, z, mine, lanes_e]
    e_copies = []
    for n in (1, 3, 2, 4, 5, 7, 6):
        yy = (y + n % 4) % NY
        cp = remote(
            se.at[yy], e_place, e_s.at[n], e_r.at[n], row_of(z, xh ^ (n // 4), c), yy * 2 + xl
        )
        cp.start()
        e_copies.append(cp)
    e_own = pltpu.make_async_copy(se.at[y], e_place, loc.at[0])
    e_own.start()

    def prep_y(i, carry):
        for ref, lo in ((k_ref, 0), (v_ref, 32)):
            full = ref[i].astype(f32)
            for cc in range(2):
                part = jnp.concatenate(
                    [full[cc * 64 : cc * 64 + 64], full[128 + cc * 64 : 192 + cc * 64]], 0
                ).T
                for h in range(H):
                    sy[h, cc, i, lo : lo + 32] = part[h * DH : (h + 1) * DH].astype(bf16)
        return carry

    lax.fori_loop(0, NR, prep_y, 0)

    y_copies = {}
    for n in (1, 2, 3, 6, 7, 4, 5):
        d, dc = n // 2, n % 2
        yy, cc = (y + d) % NY, c ^ dc
        cp = remote(
            sy.at[yy, cc], yr.at[b, rows], y_s.at[n], y_r.at[n], row_of(z, xh, cc), yy * 2 + xl
        )
        cp.start()
        y_copies[n] = cp
    y_own = pltpu.make_async_copy(sy.at[y, c], yr.at[b, rows], loc.at[2])
    y_own.start()

    place = lax.broadcasted_iota(jnp.int32, (16, QB), 0)

    def prep_x(i, carry):
        qt = q_ref[i].astype(f32).T
        d_out = do_ref[i].astype(f32)
        dt = d_out.T
        prod = (d_out * o_ref[i].astype(f32)).T
        for h in range(H):
            hs = slice(h * DH, (h + 1) * DH)
            l1, l2, l3 = pieces((lse_ref[i, h : h + 1, :] + SHIFT) * LOG2E)
            d1, d2, d3 = pieces(jnp.sum(prod[hs], axis=0, keepdims=True))
            aux = jnp.where(place == 6, 1.0, 0.0)
            for n, piece in enumerate((l1, l2, l3, d1, d2, d3)):
                aux = jnp.where(place == n, piece, aux)
            sx[h, i, 0:32] = qt[hs].astype(bf16)
            sx[h, i, 32:64] = dt[hs].astype(bf16)
            sx[h, i, 64:80] = aux.astype(bf16)
        return carry

    lax.fori_loop(0, NR, prep_x, 0)

    def piece_on(hf, step, xx, to_right=True, to_left=True):
        out = []
        for go, zz, s_sem, r_sem, row in (
            (to_right, (z + NZ - step) % NZ, fr_s, fr_r, right),
            (to_left, (z + step) % NZ, fl_s, fl_r, left),
        ):
            if go:
                part = er.at[hf, zz, aligned(xx * 64, 64)]
                cp = remote(part, part, s_sem.at[hf, step, xx], r_sem.at[hf, step, xx], row, b)
                cp.start()
                out.append(cp)
        done.extend(out)
        return out

    def ring(hf, step, before):
        if step < 3:
            out = []
            for n, xx in enumerate((xh, 1 - xh)):
                arrived(before[n])
                out.append(piece_on(hf, step, xx))
            return out
        for pair in before:
            arrived(pair)
        return [piece_on(hf, 3, 0, to_left=False), piece_on(hf, 3, 1, to_right=False)]

    def arrived(pair):
        for cp in pair:
            cp.wait_recv()

    w_copies, c_copies = [], []

    def pass_y(d):
        if d == 0:
            y_own.wait()
        else:
            y_copies[2 * d].wait_recv()
        y_copies[2 * d + 1].wait_recv()
        part = yr.at[((y + NY - d) % NY) * 2 + xl]
        cp = remote(part, part, w_s.at[d], w_r.at[d], r, y * 2 + (1 - xl))
        cp.start()
        w_copies.append(cp)

    def pass_x(d):
        if d == 0:
            x_own.wait()
        else:
            x_copies[d].wait_recv()
        part = xr.at[rows, 32:112, aligned(((y + NY - d) % NY) * QB, QB)]
        cp = remote(part, part, c_s.at[d], c_r.at[d], other, b)
        cp.start()
        c_copies.append(cp)

    for cp in e_copies[:3]:
        cp.wait_recv()
    e_own.wait()
    first = [piece_on(0, 0, xh)]
    for cp in e_copies[3:]:
        cp.wait_recv()
    first.append(piece_on(0, 0, 1 - xh))
    second = ring(1, 0, ((), ()))
    x_copies = {}
    for d in (1, 3, 2):
        yy = (y + d) % NY
        cp = remote(sx.at[yy], xr.at[rows, 32:112, lanes], x_s.at[d], x_r.at[d], r, yy * 2 + xl)
        cp.start()
        x_copies[d] = cp
    x_own = pltpu.make_async_copy(sx.at[y], xr.at[rows, 32:112, lanes], loc.at[1])
    x_own.start()

    for zz in range(NZ):
        m = mask_ref[:, zz * QB : (zz + 1) * QB]
        m0 = jnp.concatenate([m[:, 0:64], m[:, 128:192]], 1)
        m1 = jnp.concatenate([m[:, 64:128], m[:, 192:256]], 1)
        neg[zz] = jnp.where(jnp.where(c == 0, m0, m1) == 1, 0.0, NEG)

    def blank(i, carry):
        xr[i, 112:128, :] = jnp.zeros((16, NJ), bf16)
        return carry

    lax.fori_loop(0, 2 * NR, blank, 0)

    spot = lax.broadcasted_iota(jnp.int32, (32, KB), 0)
    zero = jnp.zeros((32, KB), bf16)
    aux_d = jnp.where((spot >= 3) & (spot < 6), -1.0, 0.0).astype(bf16)

    def left_operands(zz):
        aux_t = jnp.where(spot < 3, -1.0, jnp.where(spot == 6, neg[zz], 0.0)).astype(bf16)

        def left_operand(i, carry):
            both = yr[zz, i]
            scaled = both[0:32].astype(f32) * (SCALE * LOG2E)
            high = scaled.astype(bf16)
            low = (scaled - high.astype(f32)).astype(bf16)
            lhs_t = jnp.concatenate([high, low, zero, aux_t], 0)
            lhs_d = jnp.concatenate([zero, zero, both[32:64], aux_d], 0)
            lt[zz, i] = jnp.concatenate([lhs_t, lhs_d], 1).T
            return carry

        lax.fori_loop(0, 2 * NR, left_operand, 0)

    def source(d):
        return (y + NY - d) % NY

    pass_y(0)
    pass_x(0)
    left_operands(y * 2 + xl)
    first = ring(0, 1, first)
    second = ring(1, 1, second)
    pass_y(1)
    pass_y(3)
    left_operands(source(1) * 2 + xl)
    first = ring(0, 2, first)
    second = ring(1, 2, second)
    pass_y(2)
    left_operands(source(3) * 2 + xl)
    left_operands(source(2) * 2 + xl)
    pass_x(1)
    pass_x(3)
    w_copies[0].wait_recv()
    left_operands(source(0) * 2 + (1 - xl))
    first = ring(0, 3, first)
    second = ring(1, 3, second)
    pass_x(2)
    for n, d in ((1, 1), (2, 3), (3, 2)):
        w_copies[n].wait_recv()
        left_operands(source(d) * 2 + (1 - xl))
    for cp in c_copies:
        cp.wait_recv()

    def twice(i, carry):
        xr[i, 0:32, :] = xr[i, 32:64, :]
        return carry

    lax.fori_loop(0, 2 * NR, twice, 0)
    for pair in first:
        arrived(pair)
    blocks = [((z + 4 - m) % NZ, (z + 4 + m) % NZ if m else z) for m in range(4)]

    last = (((1,), (1,)), ((), ()))

    def score_rows(hf, m, z_a, z_b):
        gb[...] = jnp.zeros_like(gb)

        def one_row(i, carry):
            kt = jnp.concatenate([yr[z_a, i, 0:32], yr[z_b, i, 0:32]], 1)
            x = xr[i, :, hf * HJ : (hf + 1) * HJ]
            left = jnp.concatenate([lt[z_a, i], lt[z_b, i]], 0)
            td = jnp.dot(left, x, preferred_element_type=f32)
            e = jnp.concatenate([er[hf, z_a], er[hf, z_b]], 0).astype(f32)
            p = jnp.exp2(jnp.concatenate([td[0:KB], td[2 * KB : 3 * KB]], 0)) * e
            ds = p * jnp.concatenate([td[KB : 2 * KB], td[3 * KB :]], 0)
            gb[...] += ds
            pb, db = p.astype(bf16), ds.astype(bf16)
            gv = lax.dot_general(x[64:96], pb, last, preferred_element_type=f32)
            gk = lax.dot_general(x[0:32], db, last, preferred_element_type=f32)
            gq = jnp.dot(kt, db, preferred_element_type=f32)
            if m == 0:
                gqa[hf, i] = gq
            else:
                gqa[hf, i] += gq
            both = jnp.concatenate([gk * SCALE, gv], 0)
            if hf == 0:
                gka[m, i] = both
            else:
                out = (gka[m, i] + both).astype(bf16)
                sg[m, 0, i] = out[:, :KB]
                sg[m, 1, i] = out[:, KB:]
            return carry

        lax.fori_loop(0, 2 * NR, one_row, 0, unroll=2)

    def send_or_keep(is_self, src, dst, s_sem, r_sem, row, key):
        @pl.when(jnp.logical_not(is_self))
        def _():
            remote(src, dst, s_sem, r_sem, row, key).start()

        @pl.when(is_self)
        def _():
            cp = pltpu.make_async_copy(src, dst, loc.at[3])
            cp.start()
            cp.wait()

        later.append((is_self, src, dst, s_sem, r_sem, row, key))

    later = []

    parts = [(half, cc) for half in range(2) for cc in range(2)]

    def keys_part(ref, m, half, cc):
        return ref.at[m, half, cc * NR : (cc + 1) * NR]

    def keys_aside(m, half, cc):
        return remote(
            keys_part(sg, m, half, cc), keys_part(pr, m, half, cc),
            p_s.at[m, half, cc], p_r.at[m, half, cc], r, y * 2 + (1 - xl),
        )

    def keys_home(m, half, cc):
        src, dst = keys_part(sg, m, half, cc), gkvr.at[y * 2 + c]
        zz = blocks[m][half]
        return (
            (zz == b) & (c == cc), src, dst,
            g_s.at[m, half, cc], g_r.at[y * 2 + c], row_of(z, xh, cc), zz,
        )

    def return_aside(m):
        @pl.when(xl != (z + m) % 2)
        def _():
            for half, cc in parts:
                keys_aside(m, half, cc).start()

    def return_home(m):
        @pl.when(xl == (z + m) % 2)
        def _():
            for half, cc in parts:
                keys_aside(m, half, cc).wait_recv()
                at = slice(cc * NR, (cc + 1) * NR)
                total = sg[m, half, at].astype(f32) + pr[m, half, at].astype(f32)
                sg[m, half, at] = total.astype(bf16)
                is_self, *copy = keys_home(m, half, cc)

                @pl.when(jnp.logical_not(is_self))
                def _(copy=copy):
                    remote(*copy).start()

                @pl.when(is_self)
                def _(copy=copy):
                    cp = pltpu.make_async_copy(copy[0], copy[1], loc.at[3])
                    cp.start()
                    cp.wait()

    def return_drain(m):
        @pl.when(xl != (z + m) % 2)
        def _():
            for half, cc in parts:
                keys_aside(m, half, cc).wait_send()

        @pl.when(xl == (z + m) % 2)
        def _():
            for half, cc in parts:
                is_self, *copy = keys_home(m, half, cc)

                @pl.when(jnp.logical_not(is_self))
                def _(copy=copy):
                    remote(*copy).wait_send()

    def reduce_step(hf, m, before):
        if m == 0:
            own[hf] = gb[KB:, :]
            sr[hf, 0, 0:64] = gb[0:64, :].astype(bf16)
            sl[hf, 0, 64:128] = gb[64:128, :].astype(bf16)
            pick_r, pick_l = (hf, 0, slice(0, 64)), (hf, 0, slice(64, 128))
        else:
            arrived(before)
            if m == 1:
                sr[hf, m, 0:64] = (gb[0:64, :] + rr[hf, 0, 0:64].astype(f32)).astype(bf16)
                sr[hf, m, 64:128] = gb[64:128, :].astype(bf16)
                sl[hf, m, 0:64] = gb[128:192, :].astype(bf16)
                sl[hf, m, 64:128] = (gb[192:256, :] + rl[hf, 0, 64:128].astype(f32)).astype(bf16)
            else:
                sr[hf, m] = (gb[0:KB, :] + rr[hf, m - 1].astype(f32)).astype(bf16)
                sl[hf, m] = (gb[KB:, :] + rl[hf, m - 1].astype(f32)).astype(bf16)
            pick_r = pick_l = (hf, m)
        cr = remote(sr.at[pick_r], rr.at[pick_r], rr_s.at[hf, m], rr_r.at[hf, m], right, b)
        cl = remote(sl.at[pick_l], rl.at[pick_l], rl_s.at[hf, m], rl_r.at[hf, m], left, b)
        cr.start()
        cl.start()
        done.extend((cr, cl))
        return cr, cl

    theirs = pl.ds((1 - c) * NR, NR)

    def query_across(hf):
        cp = remote(gqa.at[hf, theirs], gqc.at[hf], qc_s.at[hf], qc_r.at[hf], other, b)
        cp.start()
        done.append(cp)
        return cp

    def query_back(hf, cp):
        cp.wait_recv()

        def add_q(i, carry):
            total = ((gqa[hf, c * NR + i] + gqc[hf, i]) * SCALE).astype(bf16)
            for n in range(2):
                sgq[2 * hf + n, i] = total[:, n * QB : (n + 1) * QB]
            return carry

        lax.fori_loop(0, NR, add_q, 0)
        for n in range(2):
            yy = 2 * hf + n
            send_or_keep(
                y == yy, sgq.at[yy], gqr.at[y], qy_s.at[yy], qy_r.at[y], r, yy * 2 + xl
            )

    def bias_back(hf, pair):
        arrived(pair)
        total = own[hf] + rr[hf, 3].astype(f32) + rl[hf, 3].astype(f32)
        total = total.astype(bf16)
        for xx in range(2):
            for n in range(2):
                yy = 2 * hf + n
                sb[xx, yy] = total[xx * 64 : (xx + 1) * 64, n * QB : (n + 1) * QB]
                send_or_keep(
                    (y == yy) & (xh == xx), sb.at[xx, yy], gbr.at[y, xh],
                    b_s.at[xx, yy], b_r.at[y, xh], row_of(z, xx, c), yy * 2 + xl,
                )

    reduced = [None, None]
    order = ((0, 0), (1, 0), (0, 1), (1, 1), (0, 2), (1, 2), (0, 3), (1, 3))
    for n, (hf, m) in enumerate(order):
        score_rows(hf, m, *blocks[m])
        if hf == 1:
            return_aside(m)
        reduced[hf] = reduce_step(hf, m, reduced[hf])
        if n == 0:
            for pair in second:
                arrived(pair)
        if n in (3, 5, 7):
            return_home((n - 3) // 2)
        if n == 6:
            q_pass = query_across(0)
    q_pass_1 = query_across(1)
    query_back(0, q_pass)
    bias_back(0, reduced[0])
    query_back(1, q_pass_1)
    bias_back(1, reduced[1])
    return_home(3)

    for n in range(8):

        @pl.when(n != y * 2 + c)
        def _(n=n):
            remote(sg.at[0, 0, 0:NR], gkvr.at[n], g_s.at[0, 0, 0], g_r.at[n], r, b).wait_recv()

    for n in range(NY):

        @pl.when(n != y)
        def _(n=n):
            remote(sgq.at[0], gqr.at[n], qy_s.at[0], qy_r.at[n], r, b).wait_recv()

        for xx in range(2):

            @pl.when((n != y) | (xx != xh))
            def _(n=n, xx=xx):
                remote(sb.at[0, 0], gbr.at[n, xx], b_s.at[0, 0], b_r.at[n, xx], r, b).wait_recv()

    for m in range(4):
        return_drain(m)

    for is_self, *copy in later:

        @pl.when(jnp.logical_not(is_self))
        def _(copy=copy):
            remote(*copy).wait_send()

    done.extend((*e_copies, *w_copies, *c_copies))
    for cp in (*done, *y_copies.values(), *x_copies.values()):
        cp.wait_send()


def home(gqr, gkvr, gbr, gq_ref, gk_ref, gv_ref, gb_ref):
    gq_ref[0] = jnp.concatenate([gqr[h, 0].astype(f32) for h in range(H)], 0).T
    for cc in range(2):
        for ref, lo in ((gk_ref, 0), (gv_ref, 32)):
            heads = [
                gkvr[h * 2 + cc, 0, lo : lo + 32].astype(f32) for h in range(H)
            ]
            part = jnp.concatenate(heads, 0).T
            ref[0, cc * 64 : cc * 64 + 64] = part[0:64]
            ref[0, 128 + cc * 64 : 192 + cc * 64] = part[64:128]

    @pl.when(pl.program_id(0) == 0)
    def _():
        for h in range(H):
            gb_ref[h] = gbr[h, 0].astype(f32) + gbr[h, 1].astype(f32)


def per_device(query, key_in, value, output, dout, lse, bias, mask):
    dma = pltpu.SemaphoreType.DMA
    vmem = pl.BlockSpec(memory_space=pltpu.VMEM)
    scratch = [
        pltpu.VMEM((H, 64, QB), bf16),
        pltpu.VMEM((H, NR, 80, QB), bf16),
        pltpu.VMEM((H, 2, NR, 64, KB), bf16),
        pltpu.VMEM((2, NZ, KB, HJ), bf16),
        pltpu.VMEM((2 * NR, 128, NJ), bf16),
        pltpu.VMEM((NZ, 2 * NR, 64, KB), bf16),
        pltpu.VMEM((NZ, 1, KB), f32),
        pltpu.VMEM((NZ, 2 * NR, 2 * KB, 128), bf16),
        pltpu.VMEM((2 * KB, HJ), f32),
        pltpu.VMEM((2, KB, HJ), f32),
        pltpu.VMEM((2, 4, KB, HJ), bf16),
        pltpu.VMEM((2, 4, KB, HJ), bf16),
        pltpu.VMEM((2, 4, KB, HJ), bf16),
        pltpu.VMEM((2, 4, KB, HJ), bf16),
        pltpu.VMEM((2, 2 * NR, DH, HJ), f32),
        pltpu.VMEM((4, 2 * NR, 64, 2 * KB), f32),
        pltpu.VMEM((4, 2, 2 * NR, 64, KB), bf16),
        pltpu.VMEM((4, 2, 2 * NR, 64, KB), bf16),
        pltpu.VMEM((2, NR, DH, HJ), f32),
        pltpu.VMEM((NY, NR, DH, QB), bf16),
        pltpu.VMEM((2, NY, 64, QB), bf16),
    ]
    four, pair, ring = dma((4,)), dma((2, 4)), dma((2, 4, 2))
    sems = [
        dma((8,)), dma((8,)), four, four, four, four, dma((8,)), dma((8,)), four, four,
        ring, ring, ring, ring,
        pair, pair, pair, pair, dma((4, 2, 2)), dma((4, 2, 2)), dma((4, 2, 2)), dma((8,)), dma((2,)), dma((2,)),
        four, four, pair, dma((4, 2)), four,
    ]
    gqr, gkvr, gbr = pl.pallas_call(
        kernel,
        out_shape=[
            jax.ShapeDtypeStruct((NY, NR, DH, QB), bf16),
            jax.ShapeDtypeStruct((8, NR, 64, KB), bf16),
            jax.ShapeDtypeStruct((NY, 2, 64, QB), bf16),
        ],
        in_specs=[vmem] * 8,
        out_specs=[vmem] * 3,
        scratch_shapes=scratch + sems,
        compiler_params=pltpu.CompilerParams(
            collective_id=0, has_side_effects=True, vmem_limit_bytes=56 << 20
        ),
    )(
        query, key_in, value, output, dout,
        lse.transpose(1, 0, 2), bias.transpose(0, 2, 1), mask.reshape(1, -1),
    )
    grad = jax.ShapeDtypeStruct(query.shape, f32)
    grad_spec = pl.BlockSpec((1, QB, H * DH), lambda i: (i, 0, 0))
    gq, gk, gv, gb = pl.pallas_call(
        home,
        grid=(NR,),
        out_shape=[grad, grad, grad, jax.ShapeDtypeStruct((H, 64, QB), f32)],
        in_specs=[
            pl.BlockSpec((NY, 1, DH, QB), lambda i: (0, i, 0, 0)),
            pl.BlockSpec((8, 1, 64, KB), lambda i: (0, i, 0, 0)),
            pl.BlockSpec((NY, 2, 64, QB), lambda i: (0, 0, 0, 0)),
        ],
        out_specs=[grad_spec] * 3 + [pl.BlockSpec((H, 64, QB), lambda i: (0, 0, 0))],
    )(gqr, gkvr, gbr)
    return gq, gk, gv, gb.transpose(0, 2, 1)


def solution(mesh):
    in_specs = (
        P("row", "key", None),
        P("row", "key", None),
        P("row", "key", None),
        P("row", "key", None),
        P("row", "key", None),
        P(None, "row", "key"),
        P(None, "key", "row"),
        P(),
    )
    out_specs = (
        P("row", "key", None),
        P("row", "key", None),
        P("row", "key", None),
        P(None, "key", "row"),
    )
    return jax.shard_map(
        per_device, mesh=mesh, in_specs=in_specs, out_specs=out_specs, check_vma=False
    )
```

time: 806 us -> 97.6 us (0.12)
  waiting for transfers between devices: 593 us -> 0 us
  matrix products: 122 us -> 0 us
  Pallas kernels: 0 us -> 96.4 us
  local copies, waits for them, and re-layouts: 68.8 us -> 0 us
  between operations: 14.2 us -> 0.64 us
    reduce_scatter x3 -> x0, waiting for transfers between devices: 376 us -> none  [the longest x1 154 us: reduce_bias(): lax.psum_scatter(partial_bias, 'row', scatter_dimension=2, tiled=True)]
    all_gather x3 -> x0, waiting for transfers between devices: 216 us -> none  [the longest x1 99.1 us: per_device(): bias_full = lax.all_gather(bias, 'row', axis=2, tiled=True)]
    dot_general x25 -> x0, matrix products: 122 us -> none  [the longest x5 45.7 us: row_scores(): jnp.einsum('qhd,khd->hqk', d_heads, v_heads, preferred_element_type=jnp.f...]
    pallas_call x0 -> x2, Pallas kernels: none -> 96.4 us  [the longest x1 91.7 us: per_device(): pl.pallas_call(kernel, out_shape=[jax.ShapeDtypeStruct((NY, NR, DH, QB),...]
    while x11 -> x0, local copies, waits for them, and re-layouts: 18.5 us -> none
    dynamic_update_slice x30 -> x0, local copies, waits for them, and re-layouts: 17.9 us -> none  [per_device(): lax.scan(one_row, jnp.zeros((head_count, col_count, piece_len), jnp.float...]
    unnamed x6 -> x0, local copies, waits for them, and re-layouts: 17.8 us -> none
    dynamic_slice x20 -> x0, local copies, waits for them, and re-layouts: 11.1 us -> none  [per_device(): lax.scan(one_row, jnp.zeros((head_count, col_count, piece_len), jnp.float...]
  transfers between devices with their start and end apart: 6 -> 0, of which waited for: 6 -> 0; matrix products, arithmetic and copies ran while one was open for 3% -> 0% of each run, Pallas kernels for 0% -> 0%
where the time goes in v2:
time: 97.6 us; the launch traced here: 97 us
  Pallas kernels  96.4 us (99%)
    pallas_call x1, Pallas kernels, per_device(): pl.pallas_call(kernel, out_shape=[jax.ShapeDtypeStruct((NY, NR, DH, QB),...  91.7 us
    pallas_call x1, Pallas kernels, per_device(): pl.pallas_call(home, grid=(NR,), out_shape=[grad, grad, grad, jax.ShapeDt...  4.68 us

profile of v2, /device:TPU:3, one launch (start us, length us, event | category | flops | bytes accessed | tf_op | source)
XLA Modules:
  0.0 97.0 jit_solution(4415066918683532634)
XLA Ops:
  0.6 91.7 %shard_map.111 = (bf16[4,5,32,256]{3,2,1,0:T(8,128)(2,1)}, bf16[8,5,64,128]{3,2,1,0:T(8,128)(2,1)}, bf16[4,2,64,256]{3,2,1,0:T(8,128)(2,1)}) custom-call(bf16[5,256,128]{2,1,0:T(8,128)(2,1)} %q_ref.1, bf16[5,256,128]{2,1,0:T(8,128)(2,1)} %k_ref.1, bf16[5,256,128]{2,1,0:T(8,128)(2,1)} %v_ref.1, bf16[5,256,128]{2,1,0:T(8,128)(2,1)} %o_ref.1, ...), custom_call_target="tpu_custom_call" | custom-call | tf_op jit(solution)/shard_map/pallas_call | solution.py:548
  92.4 4.7 %shard_map.112 = (f32[5,256,128]{2,1,0:T(8,128)}, f32[5,256,128]{2,1,0:T(8,128)}, f32[5,256,128]{2,1,0:T(8,128)}, f32[4,64,256]{2,1,0:T(8,128)}) custom-call(bf16[4,5,32,256]{3,2,1,0:T(8,128)(2,1)} %get-tuple-element.11.gqr, bf16[8,5,64,128]{3,2,1,0:T(8,128)(2,1)} %get-tuple-element.12.gkvr, bf16[4,2,64,256]{3,2,1,0:T(8,128)(2,1)} %get-tuple-element.13.gbr), custom_call_target="tpu_custom_call" | custom-call | tf_op jit(solution)/shard_map/pallas_call | solution.py:567

commit v3 on v2

--- a/solution.py
+++ b/solution.py
@@ -34,7 +34,7 @@
 def kernel(
     q_ref, k_ref, v_ref, o_ref, do_ref, lse_ref, bias_ref, mask_ref,
     gqr, gkvr, gbr,
-    se, sx, sy, er, xr, yr, neg, lt, gb, own, sr, sl, rr, rl, gqa, gka, sg, pr, gqc, sgq, sb,
+    se, sx, sy, er, xr, yr, neg, lt, gb, sr, sl, rr, rl, gqa, gka, sg, pr, gqc, sgq, sb,
     e_s, e_r, x_s, x_r, c_s, c_r, y_s, y_r, w_s, w_r, fr_s, fr_r, fl_s, fl_r,
     rr_s, rr_r, rl_s, rl_r, p_s, p_r, g_s, g_r, qc_s, qc_r, qy_s, qy_r, b_s, b_r, loc,
 ):
@@ -247,8 +247,8 @@
     pass_y(3)
     left_operands(source(1) * 2 + xl)
     first = ring(0, 2, first)
+    pass_y(2)
     second = ring(1, 2, second)
-    pass_y(2)
     left_operands(source(3) * 2 + xl)
     left_operands(source(2) * 2 + xl)
     pass_x(1)
@@ -256,7 +256,6 @@
     w_copies[0].wait_recv()
     left_operands(source(0) * 2 + (1 - xl))
     first = ring(0, 3, first)
-    second = ring(1, 3, second)
     pass_x(2)
     for n, d in ((1, 1), (2, 3), (3, 2)):
         w_copies[n].wait_recv()
@@ -269,14 +268,12 @@
         return carry
 
     lax.fori_loop(0, 2 * NR, twice, 0)
-    for pair in first:
-        arrived(pair)
     blocks = [((z + 4 - m) % NZ, (z + 4 + m) % NZ if m else z) for m in range(4)]
 
     last = (((1,), (1,)), ((), ()))
 
     def score_rows(hf, m, z_a, z_b):
-        gb[...] = jnp.zeros_like(gb)
+        gb[hf, m] = jnp.zeros((2 * KB, HJ), f32)
 
         def one_row(i, carry):
             kt = jnp.concatenate([yr[z_a, i, 0:32], yr[z_b, i, 0:32]], 1)
@@ -286,12 +283,12 @@
             e = jnp.concatenate([er[hf, z_a], er[hf, z_b]], 0).astype(f32)
             p = jnp.exp2(jnp.concatenate([td[0:KB], td[2 * KB : 3 * KB]], 0)) * e
             ds = p * jnp.concatenate([td[KB : 2 * KB], td[3 * KB :]], 0)
-            gb[...] += ds
+            gb[hf, m] += ds
             pb, db = p.astype(bf16), ds.astype(bf16)
             gv = lax.dot_general(x[64:96], pb, last, preferred_element_type=f32)
             gk = lax.dot_general(x[0:32], db, last, preferred_element_type=f32)
             gq = jnp.dot(kt, db, preferred_element_type=f32)
-            if m == 0:
+            if m == 1:
                 gqa[hf, i] = gq
             else:
                 gqa[hf, i] += gq
@@ -304,7 +301,7 @@
                 sg[m, 1, i] = out[:, KB:]
             return carry
 
-        lax.fori_loop(0, 2 * NR, one_row, 0, unroll=2)
+        lax.fori_loop(0, 2 * NR, one_row, 0, unroll=2 * NR)
 
     def send_or_keep(is_self, src, dst, s_sem, r_sem, row, key):
         @pl.when(jnp.logical_not(is_self))
@@ -382,21 +379,21 @@
                     remote(*copy).wait_send()
 
     def reduce_step(hf, m, before):
+        low, high = slice(0, 64), slice(64, KB)
         if m == 0:
-            own[hf] = gb[KB:, :]
-            sr[hf, 0, 0:64] = gb[0:64, :].astype(bf16)
-            sl[hf, 0, 64:128] = gb[64:128, :].astype(bf16)
-            pick_r, pick_l = (hf, 0, slice(0, 64)), (hf, 0, slice(64, 128))
+            sr[hf, 0, low] = gb[hf, 0, 0:64].astype(bf16)
+            sl[hf, 0, high] = gb[hf, 0, 64:128].astype(bf16)
+            pick_r, pick_l = (hf, 0, low), (hf, 0, high)
         else:
             arrived(before)
             if m == 1:
-                sr[hf, m, 0:64] = (gb[0:64, :] + rr[hf, 0, 0:64].astype(f32)).astype(bf16)
-                sr[hf, m, 64:128] = gb[64:128, :].astype(bf16)
-                sl[hf, m, 0:64] = gb[128:192, :].astype(bf16)
-                sl[hf, m, 64:128] = (gb[192:256, :] + rl[hf, 0, 64:128].astype(f32)).astype(bf16)
+                sr[hf, m, low] = (gb[hf, m, 0:64] + rr[hf, 0, low].astype(f32)).astype(bf16)
+                sr[hf, m, high] = gb[hf, m, 64:128].astype(bf16)
+                sl[hf, m, low] = gb[hf, m, 128:192].astype(bf16)
+                sl[hf, m, high] = (gb[hf, m, 192:256] + rl[hf, 0, high].astype(f32)).astype(bf16)
             else:
-                sr[hf, m] = (gb[0:KB, :] + rr[hf, m - 1].astype(f32)).astype(bf16)
-                sl[hf, m] = (gb[KB:, :] + rl[hf, m - 1].astype(f32)).astype(bf16)
+                sr[hf, m] = (gb[hf, m, 0:KB] + rr[hf, m - 1].astype(f32)).astype(bf16)
+                sl[hf, m] = (gb[hf, m, KB:] + rl[hf, m - 1].astype(f32)).astype(bf16)
             pick_r = pick_l = (hf, m)
         cr = remote(sr.at[pick_r], rr.at[pick_r], rr_s.at[hf, m], rr_r.at[hf, m], right, b)
         cl = remote(sl.at[pick_l], rl.at[pick_l], rl_s.at[hf, m], rl_r.at[hf, m], left, b)
@@ -431,7 +428,7 @@
 
     def bias_back(hf, pair):
         arrived(pair)
-        total = own[hf] + rr[hf, 3].astype(f32) + rl[hf, 3].astype(f32)
+        total = gb[hf, 0, KB:] + rr[hf, 3].astype(f32) + rl[hf, 3].astype(f32)
         total = total.astype(bf16)
         for xx in range(2):
             for n in range(2):
@@ -442,24 +439,33 @@
                     b_s.at[xx, yy], b_r.at[y, xh], row_of(z, xx, c), yy * 2 + xl,
                 )
 
+    order = ((0, 1), (1, 1), (0, 0), (1, 0), (0, 2), (1, 2), (0, 3), (1, 3))
+    sums = {2: ((0, 0),), 3: ((1, 0), (0, 1)), 4: ((1, 1),), 5: ((0, 2),), 6: ((1, 2), (0, 3)), 7: ((1, 3),)}
     reduced = [None, None]
-    order = ((0, 0), (1, 0), (0, 1), (1, 1), (0, 2), (1, 2), (0, 3), (1, 3))
     for n, (hf, m) in enumerate(order):
         score_rows(hf, m, *blocks[m])
         if hf == 1:
             return_aside(m)
-        reduced[hf] = reduce_step(hf, m, reduced[hf])
+        for part in sums.get(n, ()):
+            reduced[part[0]] = reduce_step(*part, reduced[part[0]])
         if n == 0:
+            second = ring(1, 3, second)
+        if n == 1:
+            for pair in first:
+                arrived(pair)
+        if n == 2:
             for pair in second:
                 arrived(pair)
-        if n in (3, 5, 7):
-            return_home((n - 3) // 2)
+        if n == 4:
+            return_home(1)
         if n == 6:
+            return_home(0)
             q_pass = query_across(0)
     q_pass_1 = query_across(1)
+    return_home(2)
     query_back(0, q_pass)
+    query_back(1, q_pass_1)
     bias_back(0, reduced[0])
-    query_back(1, q_pass_1)
     bias_back(1, reduced[1])
     return_home(3)
 
@@ -496,20 +502,16 @@
 
 
 def home(gqr, gkvr, gbr, gq_ref, gk_ref, gv_ref, gb_ref):
-    gq_ref[0] = jnp.concatenate([gqr[h, 0].astype(f32) for h in range(H)], 0).T
-    for cc in range(2):
-        for ref, lo in ((gk_ref, 0), (gv_ref, 32)):
-            heads = [
-                gkvr[h * 2 + cc, 0, lo : lo + 32].astype(f32) for h in range(H)
-            ]
-            part = jnp.concatenate(heads, 0).T
-            ref[0, cc * 64 : cc * 64 + 64] = part[0:64]
-            ref[0, 128 + cc * 64 : 192 + cc * 64] = part[64:128]
-
-    @pl.when(pl.program_id(0) == 0)
-    def _():
-        for h in range(H):
-            gb_ref[h] = gbr[h, 0].astype(f32) + gbr[h, 1].astype(f32)
+    for i in range(NR):
+        gq_ref[i] = jnp.concatenate([gqr[h, i].astype(f32) for h in range(H)], 0).T
+        for cc in range(2):
+            for ref, lo in ((gk_ref, 0), (gv_ref, 32)):
+                heads = [gkvr[h * 2 + cc, i, lo : lo + 32].astype(f32) for h in range(H)]
+                part = jnp.concatenate(heads, 0).T
+                ref[i, cc * 64 : cc * 64 + 64] = part[0:64]
+                ref[i, 128 + cc * 64 : 192 + cc * 64] = part[64:128]
+    for h in range(H):
+        gb_ref[h] = gbr[h, 0].astype(f32) + gbr[h, 1].astype(f32)
 
 
 def per_device(query, key_in, value, output, dout, lse, bias, mask):
@@ -524,8 +526,7 @@
         pltpu.VMEM((NZ, 2 * NR, 64, KB), bf16),
         pltpu.VMEM((NZ, 1, KB), f32),
         pltpu.VMEM((NZ, 2 * NR, 2 * KB, 128), bf16),
-        pltpu.VMEM((2 * KB, HJ), f32),
-        pltpu.VMEM((2, KB, HJ), f32),
+        pltpu.VMEM((2, 4, 2 * KB, HJ), f32),
         pltpu.VMEM((2, 4, KB, HJ), bf16),
         pltpu.VMEM((2, 4, KB, HJ), bf16),
         pltpu.VMEM((2, 4, KB, HJ), bf16),
@@ -563,17 +564,11 @@
         lse.transpose(1, 0, 2), bias.transpose(0, 2, 1), mask.reshape(1, -1),
     )
     grad = jax.ShapeDtypeStruct(query.shape, f32)
-    grad_spec = pl.BlockSpec((1, QB, H * DH), lambda i: (i, 0, 0))
     gq, gk, gv, gb = pl.pallas_call(
         home,
-        grid=(NR,),
         out_shape=[grad, grad, grad, jax.ShapeDtypeStruct((H, 64, QB), f32)],
-        in_specs=[
-            pl.BlockSpec((NY, 1, DH, QB), lambda i: (0, i, 0, 0)),
-            pl.BlockSpec((8, 1, 64, KB), lambda i: (0, i, 0, 0)),
-            pl.BlockSpec((NY, 2, 64, QB), lambda i: (0, 0, 0, 0)),
-        ],
-        out_specs=[grad_spec] * 3 + [pl.BlockSpec((H, 64, QB), lambda i: (0, 0, 0))],
+        in_specs=[vmem] * 3,
+        out_specs=[vmem] * 4,
     )(gqr, gkvr, gbr)
     return gq, gk, gv, gb.transpose(0, 2, 1)
 

time: 97.6 us -> 90.4 us (0.926)
  Pallas kernels: 96.4 us -> 89.6 us
    pallas_call x1, Pallas kernels: 91.7 us -> 86.7 us  [per_device(): pl.pallas_call(kernel, out_shape=[jax.ShapeDtypeStruct((NY, NR, DH, QB),...]
    pallas_call x1, Pallas kernels: 4.68 us -> 2.91 us  [per_device(): pl.pallas_call(home, out_shape=[grad, grad, grad, jax.ShapeDtypeStruct((H...]
where the time goes in v3:
time: 90.4 us; the launch traced here: 90.3 us
  Pallas kernels  89.6 us (99%)
    pallas_call x1, Pallas kernels, per_device(): pl.pallas_call(kernel, out_shape=[jax.ShapeDtypeStruct((NY, NR, DH, QB),...  86.7 us
    pallas_call x1, Pallas kernels, per_device(): pl.pallas_call(home, out_shape=[grad, grad, grad, jax.ShapeDtypeStruct((H...  2.91 us

profile of v3, /device:TPU:3, one launch (start us, length us, event | category | flops | bytes accessed | tf_op | source)
XLA Modules:
  0.0 90.3 jit_solution(6538709801184956734)
XLA Ops:
  0.6 86.7 %shard_map.111 = (bf16[4,5,32,256]{3,2,1,0:T(8,128)(2,1)}, bf16[8,5,64,128]{3,2,1,0:T(8,128)(2,1)}, bf16[4,2,64,256]{3,2,1,0:T(8,128)(2,1)}) custom-call(bf16[5,256,128]{2,1,0:T(8,128)(2,1)} %q_ref.1, bf16[5,256,128]{2,1,0:T(8,128)(2,1)} %k_ref.1, bf16[5,256,128]{2,1,0:T(8,128)(2,1)} %v_ref.1, bf16[5,256,128]{2,1,0:T(8,128)(2,1)} %o_ref.1, ...), custom_call_target="tpu_custom_call" | custom-call | tf_op jit(solution)/shard_map/pallas_call | solution.py:549
  87.4 2.9 %shard_map.112 = (f32[5,256,128]{2,1,0:T(8,128)}, f32[5,256,128]{2,1,0:T(8,128)}, f32[5,256,128]{2,1,0:T(8,128)}, f32[4,64,256]{2,1,0:T(8,128)}) custom-call(bf16[4,5,32,256]{3,2,1,0:T(8,128)(2,1)} %get-tuple-element.11.gqr, bf16[8,5,64,128]{3,2,1,0:T(8,128)(2,1)} %get-tuple-element.12.gkvr, bf16[4,2,64,256]{3,2,1,0:T(8,128)(2,1)} %get-tuple-element.13.gbr), custom_call_target="tpu_custom_call" | custom-call | tf_op jit(solution)/shard_map/pallas_call | solution.py:567

commit v4 on v3

--- a/solution.py
+++ b/solution.py
@@ -310,9 +310,7 @@
 
         @pl.when(is_self)
         def _():
-            cp = pltpu.make_async_copy(src, dst, loc.at[3])
-            cp.start()
-            cp.wait()
+            dst[...] = src[...]
 
         later.append((is_self, src, dst, s_sem, r_sem, row, key))
 
@@ -359,9 +357,7 @@
 
                 @pl.when(is_self)
                 def _(copy=copy):
-                    cp = pltpu.make_async_copy(copy[0], copy[1], loc.at[3])
-                    cp.start()
-                    cp.wait()
+                    copy[1][...] = copy[0][...]
 
     def return_drain(m):
         @pl.when(xl != (z + m) % 2)

time: 90.4 us -> 90.4 us (level)
  no operation moved by 1% of the time
where the time goes in v4:
time: 90.4 us; the launch traced here: 90.3 us
  Pallas kernels  89.6 us (99%)
    pallas_call x1, Pallas kernels, per_device(): pl.pallas_call(kernel, out_shape=[jax.ShapeDtypeStruct((NY, NR, DH, QB),...  86.7 us
    pallas_call x1, Pallas kernels, per_device(): pl.pallas_call(home, out_shape=[grad, grad, grad, jax.ShapeDtypeStruct((H...  2.91 us

profile of v4, /device:TPU:3, one launch (start us, length us, event | category | flops | bytes accessed | tf_op | source)
XLA Modules:
  0.0 90.3 jit_solution(17475266747287568774)
XLA Ops:
  0.6 86.7 %shard_map.111 = (bf16[4,5,32,256]{3,2,1,0:T(8,128)(2,1)}, bf16[8,5,64,128]{3,2,1,0:T(8,128)(2,1)}, bf16[4,2,64,256]{3,2,1,0:T(8,128)(2,1)}) custom-call(bf16[5,256,128]{2,1,0:T(8,128)(2,1)} %q_ref.1, bf16[5,256,128]{2,1,0:T(8,128)(2,1)} %k_ref.1, bf16[5,256,128]{2,1,0:T(8,128)(2,1)} %v_ref.1, bf16[5,256,128]{2,1,0:T(8,128)(2,1)} %o_ref.1, ...), custom_call_target="tpu_custom_call" | custom-call | tf_op jit(solution)/shard_map/pallas_call | solution.py:545
  87.4 2.9 %shard_map.112 = (f32[5,256,128]{2,1,0:T(8,128)}, f32[5,256,128]{2,1,0:T(8,128)}, f32[5,256,128]{2,1,0:T(8,128)}, f32[4,64,256]{2,1,0:T(8,128)}) custom-call(bf16[4,5,32,256]{3,2,1,0:T(8,128)(2,1)} %get-tuple-element.11.gqr, bf16[8,5,64,128]{3,2,1,0:T(8,128)(2,1)} %get-tuple-element.12.gkvr, bf16[4,2,64,256]{3,2,1,0:T(8,128)(2,1)} %get-tuple-element.13.gbr), custom_call_target="tpu_custom_call" | custom-call | tf_op jit(solution)/shard_map/pallas_call | solution.py:563
